TPU v7x, 32 devices: a whole 2x2x4 slice. The times are simulated.
32 devices in a mesh: groups: 2 (over x), vel: 8 (over z, y), sub: 2 (over core).
Axes of the slice: x: 2, y: 2, z: 4, core: 2. Of those that a mesh axis runs over, the one named last changes fastest.
Arguments:
- dist: float32 [16, 256, 1024], P('sub', 'vel', 'groups'), parts along dimension 2, may hold values from 0 to 6, as said below
- cell_type: int32 [1024], P('groups'), parts along dimension 0, may hold values from 0 to 1, as said below
- groove_mask: int32 [64], P('groups'), parts along dimension 0, may hold values 0 or 1
Outputs:
- dist_next: float32 [16, 256, 1024], P('sub', 'vel', 'groups'), parts along dimension 2
There are 2 independent parts, one for each index of `groups`. A program takes and returns all parts, laid end to end along the dimension named above; each array names one. Nothing has to cross between parts.
Inputs may be any that keep to these rules, and one draw needn't show every extreme that they name: `cell_type`: in each column the solid cells are its lowest ones; a column holds at most a quarter of 16 of them, and every draw has columns with that many and columns with none; grooves repeat along the columns with a period of 4 to 12 columns. `dist`: every entry is positive.
All inputs are finite; a program needn't handle non-finite values.
Results may differ from a plain program's by a relative error of at most 0.0001.
Values sent between devices are 32-bit elements; how exact they have to be, the bound alone decides.
A program may use at most 128 MiB of HBM per device.

v0:
```python
import math
import jax
import jax.numpy as jnp
from jax import lax
from jax.sharding import PartitionSpec as P

VN = 16
SY = 16
STEPS = 2
VEL_RANGE = 5.0
TOP_SPEED = 1.0
ACC_LAND = 0.4
ACC_TOP = 0.7
KNUDSEN = 1.0
HIGHEST = lax.Precision.HIGHEST
FORMS = ("kj,jxzc->kxzc", "kj,yjzc->ykzc", "kj,yxjc->yxkc")


def swapped(value, axis, distance):
    mask = 2**distance
    pairs = [(source, source ^ mask) for source in range(lax.axis_size(axis))]
    return lax.ppermute(value, axis, pairs)


def spacing_of(count):
    return 2.0 * VEL_RANGE / count


def time_step(count):
    return 0.8 / ((count - 1) * spacing_of(count))


def speeds(index, count):
    return (index.astype(jnp.float32) - (count - 1) / 2.0) * spacing_of(count)


def wave_numbers(count):
    index = jnp.arange(count, dtype=jnp.int32)
    wrapped = jnp.where(index < count // 2, index, index - count)
    return wrapped.astype(jnp.float32) * (math.pi / VEL_RANGE)


def kernels(count):
    wave = wave_numbers(count)
    wave_y = wave[:, None, None]
    wave_x = wave[None, :, None]
    wave_z = wave[None, None, :]
    square = wave_y * wave_y + wave_x * wave_x + wave_z * wave_z
    first = 1.0 / (1.0 + square / 12.0)
    second = 3.0 * jnp.cos(0.9 * wave_x) / (1.0 + square / 10.0)
    damped = 1.0 + square / 9.0
    loss = 3.0 / (damped * damped)
    return (first, second, loss)


def dft_tables(count):
    index = jnp.arange(count, dtype=jnp.float32)
    angle = 2.0 * math.pi / count * index[:, None] * index[None, :]
    return (jnp.cos(angle), jnp.sin(angle))


def full_grid(count):
    index = jnp.arange(count * count * count, dtype=jnp.int32)
    velocity_y = speeds(index // (count * count), count)
    velocity_x = speeds(index // count % count, count)
    velocity_z = speeds(index % count, count)
    return (velocity_x, velocity_y, velocity_z)


def wall_tables(velocity_x, velocity_y, velocity_z):
    rest = jnp.exp(
        -(velocity_x * velocity_x + velocity_y * velocity_y + velocity_z * velocity_z) / 2.0
    )
    shifted = velocity_x - TOP_SPEED
    moving = jnp.exp(-(shifted * shifted + velocity_y * velocity_y + velocity_z * velocity_z) / 2.0)
    weights = jnp.stack(
        [
            jnp.maximum(-velocity_x, 0.0),
            jnp.maximum(velocity_x, 0.0),
            jnp.maximum(-velocity_y, 0.0),
            jnp.maximum(velocity_y, 0.0),
        ]
    )
    return (rest, moving, weights)


def wall_norms(count):
    velocity_x, velocity_y, velocity_z = full_grid(count)
    rest, moving, weights = wall_tables(velocity_x, velocity_y, velocity_z)
    return (
        jnp.sum(jnp.maximum(velocity_x, 0.0) * rest),
        jnp.sum(jnp.maximum(-velocity_x, 0.0) * rest),
        jnp.sum(jnp.maximum(velocity_y, 0.0) * rest),
        jnp.sum(jnp.maximum(-velocity_y, 0.0) * moving),
    )


def cell_masks(cell_type, groove_mask, height_count):
    total = cell_type.shape[0]
    solid = cell_type.astype(jnp.float32)
    height = jnp.arange(total, dtype=jnp.int32) % height_count
    left_solid = jnp.roll(solid, height_count)
    right_solid = jnp.roll(solid, -height_count)
    below_solid = jnp.where(height == 0, 1.0, jnp.roll(solid, 1))
    top_wall = jnp.where(height == height_count - 1, 1.0, 0.0 * solid)
    accommodation = jnp.repeat(jnp.where(groove_mask == 1, 1.0, ACC_LAND), height_count)
    return jnp.stack([left_solid, right_solid, below_solid, top_wall, accommodation, 1.0 - solid])


def advance(center, left, right, below, above, mirror, flux, masks, velocity, norms, step_size):
    velocity_x, velocity_y, rest, moving = velocity
    left_solid = masks[0][None, :]
    right_solid = masks[1][None, :]
    below_solid = masks[2][None, :]
    top_wall = masks[3][None, :]
    accommodation = masks[4][None, :]
    fluid = masks[5][None, :]
    left_ghost = (flux[0] / norms[0])[None, :] * rest
    right_ghost = (flux[1] / norms[1])[None, :] * rest
    below_ghost = (1.0 - accommodation) * mirror + accommodation * (flux[2] / norms[2])[
        None, :
    ] * rest
    above_ghost = (1.0 - ACC_TOP) * mirror + ACC_TOP * (flux[3] / norms[3])[None, :] * moving
    left_value = jnp.where(left_solid > 0.0, left_ghost, left)
    right_value = jnp.where(right_solid > 0.0, right_ghost, right)
    below_value = jnp.where(below_solid > 0.0, below_ghost, below)
    above_value = jnp.where(top_wall > 0.0, above_ghost, above)
    change = jnp.maximum(velocity_x, 0.0) * (center - left_value) + jnp.minimum(velocity_x, 0.0) * (
        right_value - center
    )
    change = (
        change
        + jnp.maximum(velocity_y, 0.0) * (center - below_value)
        + jnp.minimum(velocity_y, 0.0) * (above_value - center)
    )
    return (center - step_size * change) * fluid


def fourier_pass(real_part, imag_part, cosine, sine_table, form, forward):

    def apply(table, values):
        return jnp.einsum(form, table, values, precision=HIGHEST)

    if imag_part is None:
        return (apply(cosine, real_part), -apply(sine_table, real_part))
    if forward:
        return (
            apply(cosine, real_part) + apply(sine_table, imag_part),
            apply(cosine, imag_part) - apply(sine_table, real_part),
        )
    return (
        apply(cosine, real_part) - apply(sine_table, imag_part),
        apply(cosine, imag_part) + apply(sine_table, real_part),
    )


def collide(cube, tables, cosine, sine_table, rate):
    count = cube.shape[0]
    scale = 1.0 / (count * count * count)
    real_part, imag_part = fourier_pass(cube, None, cosine, sine_table, FORMS[0], True)
    real_part, imag_part = fourier_pass(real_part, imag_part, cosine, sine_table, FORMS[1], True)
    real_part, imag_part = fourier_pass(real_part, imag_part, cosine, sine_table, FORMS[2], True)

    def inverse(table):
        factor = table[..., None]
        first_real, first_imag = fourier_pass(
            real_part * factor, imag_part * factor, cosine, sine_table, FORMS[0], False
        )
        second_real, second_imag = fourier_pass(
            first_real, first_imag, cosine, sine_table, FORMS[1], False
        )
        last = jnp.einsum(FORMS[2], cosine, second_real, precision=HIGHEST) - jnp.einsum(
            FORMS[2], sine_table, second_imag, precision=HIGHEST
        )
        return last * scale

    gain = inverse(tables[0]) * inverse(tables[1])
    return cube + rate * (gain - cube * inverse(tables[2]))


def local(dist, cell_type, groove_mask):
    count = VN
    height_count = SY
    volume = count * count * count
    local_y, local_xz, total_cells = dist.shape
    masks = cell_masks(cell_type, groove_mask, height_count)
    norms = wall_norms(count)
    step_size = time_step(count)
    rate = step_size / KNUDSEN
    cosine, sine_table = dft_tables(count)
    tables = kernels(count)
    sub_index = lax.axis_index("sub")
    vel_index = lax.axis_index("vel")
    index_y = sub_index * local_y + jnp.arange(local_y, dtype=jnp.int32)
    index_xz = vel_index * local_xz + jnp.arange(local_xz, dtype=jnp.int32)
    block_shape = (local_y, local_xz)
    velocity_y = jnp.broadcast_to(speeds(index_y, count)[:, None], block_shape).reshape(-1)
    velocity_x = jnp.broadcast_to(speeds(index_xz // count, count)[None, :], block_shape).reshape(
        -1
    )
    velocity_z = jnp.broadcast_to(speeds(index_xz % count, count)[None, :], block_shape).reshape(-1)
    rest, moving, weights = wall_tables(velocity_x, velocity_y, velocity_z)
    velocity = (velocity_x[:, None], velocity_y[:, None], rest[:, None], moving[:, None])
    columns_total = total_cells // height_count
    depth = jnp.sum(cell_type.reshape(columns_total, height_count), axis=1)
    bottom_index = jnp.arange(columns_total, dtype=jnp.int32) * height_count + depth
    state = dist
    for iteration in range(STEPS):
        space = lax.all_to_all(
            lax.all_to_all(state, "vel", split_axis=2, concat_axis=1, tiled=True),
            "sub",
            split_axis=2,
            concat_axis=0,
            tiled=True,
        )
        cells = space.shape[2]
        post = collide(
            space.reshape(count, count, count, cells), tables, cosine, sine_table, rate
        ).reshape(volume, cells)
        back = lax.all_to_all(
            lax.all_to_all(
                post.reshape(count, count * count, 1, cells),
                "vel",
                split_axis=1,
                concat_axis=2,
                tiled=True,
            ),
            "sub",
            split_axis=0,
            concat_axis=3,
            tiled=True,
        )
        center = back.reshape(local_y * local_xz, total_cells)
        flux = lax.psum(jnp.dot(weights, center, precision=HIGHEST), ("vel", "sub"))
        shaped = center.reshape(local_y, local_xz, total_cells)
        bottom_rows = jnp.take(shaped, bottom_index, axis=2)
        top_rows = shaped[:, :, height_count - 1 :: height_count]
        outgoing = jnp.where(sub_index == 0, bottom_rows, top_rows)
        incoming = swapped(outgoing, "sub", 0)
        mirror = jnp.repeat(incoming[::-1], height_count, axis=2).reshape(
            local_y * local_xz, total_cells
        )
        result = advance(
            center,
            jnp.roll(center, height_count, 1),
            jnp.roll(center, -height_count, 1),
            jnp.roll(center, 1, 1),
            jnp.roll(center, -1, 1),
            mirror,
            flux,
            masks,
            velocity,
            norms,
            step_size,
        )
        state = result.reshape(local_y, local_xz, total_cells)
    return state


def solution(mesh):
    return jax.shard_map(
        local,
        mesh=mesh,
        in_specs=(P("sub", "vel", "groups"), P("groups"), P("groups")),
        out_specs=P("sub", "vel", "groups"),
        check_vma=False,
    )
```

profile of v0, /device:TPU:1, one launch (start us, length us, event | category | flops | bytes accessed | tf_op | source)
XLA Modules:
  0.0 529.2 jit_solution(7535001363961206787)
XLA Ops:
  3.6 6.4 %all-to-all-start = ((f32[8,1,16384]{2,1,0:T(1,128)}), f32[8,1,16384]{2,1,0:T(1,128)S(1)}, u32[]{:S(2)}, u32[]{:S(2)}) async-start(f32[8,1,16384]{2,1,0:T(1,128)} %reshape.613), calls=%async_computation | async-start | bytes 1048576 | tf_op jit(solution)/shard_map/all_to_all | solution.py:210
  19.5 3.9 all-to-all-done
  27.4 5.8 %all_to_all.132 = f32[8,256,64]{1,0,2:T(8,128)S(1)} all-to-all(f32[8,256,64]{1,0,2:T(8,128)S(1)} %copy.780), channel_id=1, replica_groups=mesh['groups'=2,'vel'=8,'sub'=2] {'sub'}, dimensions={2} | all-to-all | bytes 1048576 | tf_op jit(solution)/shard_map/all_to_all | solution.py:209
  38.6 3.3 fusion.158
  41.9 3.3 fusion.160
  45.2 3.5 subtract_bitcast_fusion.7
  53.7 3.4 add_bitcast_fusion.7
  60.0 3.4 multiply_bitcast_fusion.10
  72.4 3.4 fusion.134
  75.8 3.3 fusion.136
  88.1 3.4 fusion.102
  91.4 3.7 fusion.104
  103.9 3.5 fusion.118
  107.4 3.3 fusion.120
  113.7 3.3 subtract_bitcast_fusion.6
  117.1 3.5 add_bitcast_fusion.6
  128.6 3.8 subtract_bitcast_fusion.4
  132.4 3.4 add_bitcast_fusion.4
  144.0 3.4 subtract_bitcast_fusion.5
  147.4 3.3 add_bitcast_fusion.5
  155.9 8.6 %fusion.5 = f32[16,16,16,32]{3,0,2,1:T(8,128)} fusion(f32[16,16,16,32]{3,0,2,1:T(8,128)S(1)} %bitcast.348, f32[16,16,32,16]{2,3,1,0:T(8,128)S(1)} %fusion.23, f32[16,16,32,16]{2,3,1,0:T(8,128)S(1)} %fusion.25, f32[16,16,32,16]{2,3,1,0:T(8,128)S(1)} %fusion.29, f32[16,16,32,16]{2,3,1,0:T(8,128)S(1)} %fusion.31, f32[16,16,32,16]{2,3,1,0:T(8,128)S(1)} %fusion.34, ...), kind=kLoop, calls=%fused_computation.9 | loop fusion | flops 1441792 | bytes 4194304 | tf_op jit(solution)/shard_map/add | solution.py:178
  167.7 3.9 all-to-all-start.2
  177.5 7.6 %all-to-all-done.2 = f32[8,1,16384]{2,1,0:T(1,128)S(1)} async-done(((f32[8,1,16384]{2,1,0:T(1,128)}), f32[8,1,16384]{2,1,0:T(1,128)S(1)}, u32[]{:S(2)}, u32[]{:S(2)}) %all-to-all-start.2) | async-done | bytes 524320 | tf_op jit(solution)/shard_map/all_to_all | solution.py:221
  192.3 5.5 %all_to_all.133 = f32[2,1,65536]{2,1,0:T(1,128)S(1)} all-to-all(f32[2,1,65536]{2,1,0:T(1,128)S(1)} %reshape.617), channel_id=1, replica_groups=mesh['groups'=2,'vel'=8,'sub'=2] {'sub'}, dimensions={0} | all-to-all | bytes 1048576 | tf_op jit(solution)/shard_map/all_to_all | solution.py:220
  217.9 30.5 %psum.14 = f32[4,512]{1,0:T(4,128)} all-reduce(f32[4,512]{1,0:T(4,128)} %fusion.572), channel_id=1, replica_groups=mesh['groups'=2,'vel'=8,'sub'=2] {'vel','sub'}, use_global_device_ids=true, to_apply=%region_0.1 | all-reduce | flops 2048 | bytes 16384 | tf_op jit(solution)/shard_map/psum | solution.py:234
  254.5 4.1 slice_divide_fusion.5
  269.2 3.3 fusion.253
  275.2 16.8 %all_to_all.134 = f32[8,1,16384]{2,1,0:T(1,128)S(1)} all-to-all(f32[8,1,16384]{2,1,0:T(1,128)S(1)} %reshape.619), channel_id=1, replica_groups=mesh['groups'=2,'vel'=8,'sub'=2] {'vel'}, dimensions={0} | all-to-all | bytes 1048576 | tf_op jit(solution)/shard_map/all_to_all | solution.py:210
  295.6 4.9 all_to_all.135
  305.8 3.3 fusion.94
  312.4 3.7 subtract_bitcast_fusion.3
  321.1 3.4 add_bitcast_fusion.3
  327.2 3.4 multiply_bitcast_fusion.4
  339.6 3.4 fusion.70
  349.2 3.3 fusion.48
  355.4 3.3 fusion.38
  358.8 3.5 fusion.40
  371.1 3.6 fusion.54
  380.9 3.3 subtract_bitcast_fusion.2
  384.3 3.7 add_bitcast_fusion.2
  396.0 3.6 subtract_bitcast_fusion
  399.6 3.4 add_bitcast_fusion
  411.2 3.4 subtract_bitcast_fusion.1
  414.6 3.3 add_bitcast_fusion.1
  423.3 8.6 %fusion.2 = f32[16,16,16,32]{3,0,2,1:T(8,128)} fusion(f32[16,16,16,32]{3,0,2,1:T(8,128)S(1)} %bitcast.345, f32[16,16,32,16]{2,3,1,0:T(8,128)S(1)} %fusion.7, f32[16,16,32,16]{2,3,1,0:T(8,128)S(1)} %fusion.9, f32[16,16,32,16]{2,3,1,0:T(8,128)S(1)} %fusion.13, f32[16,16,32,16]{2,3,1,0:T(8,128)S(1)} %fusion.15, f32[16,16,32,16]{2,3,1,0:T(8,128)S(1)} %fusion.18, ...), kind=kLoop, calls=%fused_computation.5 | loop fusion | flops 1441792 | bytes 4194304 | tf_op jit(solution)/shard_map/add | solution.py:178
  434.4 17.0 %all_to_all.136 = f32[8,1,16384]{2,1,0:T(1,128)S(1)} all-to-all(f32[8,1,16384]{2,1,0:T(1,128)S(1)} %reshape.621), channel_id=1, replica_groups=mesh['groups'=2,'vel'=8,'sub'=2] {'vel'}, dimensions={0} | all-to-all | bytes 1048576 | tf_op jit(solution)/shard_map/all_to_all | solution.py:221
  458.4 5.5 %all_to_all.137 = f32[2,1,65536]{2,1,0:T(1,128)S(1)} all-to-all(f32[2,1,65536]{2,1,0:T(1,128)S(1)} %reshape.623), channel_id=1, replica_groups=mesh['groups'=2,'vel'=8,'sub'=2] {'sub'}, dimensions={0} | all-to-all | bytes 1048576 | tf_op jit(solution)/shard_map/all_to_all | solution.py:220
  481.6 29.9 %psum.15 = f32[4,512]{1,0:T(4,128)S(1)} all-reduce(f32[4,512]{1,0:T(4,128)S(1)} %fusion.571), channel_id=1, replica_groups=mesh['groups'=2,'vel'=8,'sub'=2] {'vel','sub'}, use_global_device_ids=true, to_apply=%region_6.8 | all-reduce | flops 2048 | bytes 16384 | tf_op jit(solution)/shard_map/psum | solution.py:234
  (243 shorter events, 255.7 us)
Async XLA Ops:
  1.8 11.1 %copy-start.33 = (s32[32]{0:T(128)S(1)}, s32[32]{0:T(128)}, u32[]{:S(2)}) copy-start(s32[32]{0:T(128)} %param.7) | copy-start | bytes 388
  1.8 11.1 %copy-start.12 = (s32[512]{0:T(512)S(1)}, s32[512]{0:T(512)}, u32[]{:S(2)}) copy-start(s32[512]{0:T(512)} %param.6) | copy-start | bytes 6148
  3.6 19.8 %all-to-all-start = ((f32[8,1,16384]{2,1,0:T(1,128)}), f32[8,1,16384]{2,1,0:T(1,128)S(1)}, u32[]{:S(2)}, u32[]{:S(2)}) async-start(f32[8,1,16384]{2,1,0:T(1,128)} %reshape.613), calls=%async_computation | async-start | bytes 1048576 | tf_op jit(solution)/shard_map/all_to_all | solution.py:210
  10.5 8.9 %copy-start.23 = (f32[8]{0:T(128)}, f32[8]{0:T(128)S(1)}, u32[]{:S(2)}) copy-start(f32[8]{0:T(128)S(1)} %get-tuple-element.71) | copy-start | bytes 100
  12.9 6.5 %copy-start.24 = (f32[32]{0:T(128)}, f32[32]{0:T(128)S(1)}, u32[]{:S(2)}) copy-start(f32[32]{0:T(128)S(1)} %get-tuple-element.67) | copy-start | bytes 388
  17.3 251.8 %copy-start.13 = (f32[512]{0:T(512)}, f32[512]{0:T(512)S(1)}, u32[]{:S(2)}) copy-start(f32[512]{0:T(512)S(1)} %sub.287) | copy-start | bytes 6148
  164.5 9.8 %copy-start.21 = (f32[496]{0:T(512)S(1)}, f32[496]{0:T(512)}, u32[]{:S(2)}) copy-start(f32[496]{0:T(512)} %get-tuple-element.55) | copy-start | bytes 5956
  164.5 9.8 %copy-start.22 = (f32[496]{0:T(512)S(1)}, f32[496]{0:T(512)}, u32[]{:S(2)}) copy-start(f32[496]{0:T(512)} %get-tuple-element.56) | copy-start | bytes 5956
  164.5 9.8 %copy-start.26 = (f32[16]{0:T(128)S(1)}, f32[16]{0:T(128)}, u32[]{:S(2)}) copy-start(f32[16]{0:T(128)} %get-tuple-element.53) | copy-start | bytes 196
  164.5 9.8 %copy-start.27 = (f32[16]{0:T(128)S(1)}, f32[16]{0:T(128)}, u32[]{:S(2)}) copy-start(f32[16]{0:T(128)} %get-tuple-element.54) | copy-start | bytes 196
  164.5 10.5 %copy-start.32 = (s32[32]{0:T(128)S(1)}, s32[32]{0:T(128)}, u32[]{:S(2)}) copy-start(s32[32]{0:T(128)} %get-tuple-element.11) | copy-start | bytes 388
  164.5 12.9 %copy-start.28 = (f32[8]{0:T(128)S(1)}, f32[8]{0:T(128)}, u32[]{:S(2)}) copy-start(f32[8]{0:T(128)} %get-tuple-element.72) | copy-start | bytes 100
  164.5 12.9 %copy-start.29 = (f32[32]{0:T(128)S(1)}, f32[32]{0:T(128)}, u32[]{:S(2)}) copy-start(f32[32]{0:T(128)} %get-tuple-element.63) | copy-start | bytes 388
  164.5 12.9 %copy-start.30 = (f32[32]{0:T(128)S(1)}, f32[32]{0:T(128)}, u32[]{:S(2)}) copy-start(f32[32]{0:T(128)} %get-tuple-element.64) | copy-start | bytes 388
  164.6 12.9 %copy-start.31 = (f32[32]{0:T(128)S(1)}, f32[32]{0:T(128)}, u32[]{:S(2)}) copy-start(f32[32]{0:T(128)} %get-tuple-element.68) | copy-start | bytes 388
  167.7 17.5 %all-to-all-start.2 = ((f32[8,1,16384]{2,1,0:T(1,128)}), f32[8,1,16384]{2,1,0:T(1,128)S(1)}, u32[]{:S(2)}, u32[]{:S(2)}) async-start(f32[8,1,16384]{2,1,0:T(1,128)} %reshape.615), calls=%async_computation.2 | async-start | bytes 1048576 | tf_op jit(solution)/shard_map/all_to_all | solution.py:221
  177.5 91.6 %copy-start.8 = (f32[8,32]{1,0:T(8,128)}, f32[8,32]{1,0:T(8,128)S(1)}, u32[]{:S(2)}) copy-start(f32[8,32]{1,0:T(8,128)S(1)} %get-tuple-element.57) | copy-start | bytes 3076
  177.5 91.6 %copy-start.10 = (f32[8,32]{1,0:T(8,128)}, f32[8,32]{1,0:T(8,128)S(1)}, u32[]{:S(2)}) copy-start(f32[8,32]{1,0:T(8,128)S(1)} %get-tuple-element.58) | copy-start | bytes 3076
  208.0 2.7 copy-start.1
  249.8 15.5 %copy-start.7 = (f32[256,496]{0,1:T(8,128)S(1)}, f32[256,496]{0,1:T(8,128)}, u32[]{:S(2)}) copy-start(f32[256,496]{0,1:T(8,128)} %get-tuple-element.33) | copy-start | bytes 1523716
  249.8 16.5 %copy-start.5 = (f32[256,511]{0,1:T(8,128)S(1)}, f32[256,511]{0,1:T(8,128)}, u32[]{:S(2)}) copy-start(f32[256,511]{0,1:T(8,128)} %get-tuple-element.30) | copy-start | bytes 1569796
  250.9 16.4 %copy-start.4 = (f32[256,511]{0,1:T(8,128)S(1)}, f32[256,511]{0,1:T(8,128)}, u32[]{:S(2)}) copy-start(f32[256,511]{0,1:T(8,128)} %get-tuple-element.31) | copy-start | bytes 1569796
  251.9 16.4 %collective-permute-start = (f32[8,32,32]{2,1,0:T(8,128)S(1)}, f32[8,32,32]{2,1,0:T(8,128)S(1)}, u32[]{:S(2)}, u32[]{:S(2)}) collective-permute-start(f32[8,32,32]{2,1,0:T(8,128)S(1)} %bitcast_select_fusion.1), channel_id=1, source_target_pairs={{0,1},{1,0},{2,3},{3,2},{4,5},{5,4},{6,7},{7,6},{8,9},{9,8},{10,11... | collective-permute-start | bytes 98312 | tf_op jit(solution)/shard_map/ppermute | solution.py:22
  472.1 2.2 copy-start.17
  472.1 2.2 copy-start.18
  472.1 2.2 copy-start.19
  472.1 2.2 copy-start.20
  474.8 2.1 copy-start
  479.6 32.0 %copy-start.16 = (f32[1,512]{1,0:T(1,128)S(1)}, f32[1,512]{1,0:T(1,128)}, u32[]{:S(2)}) copy-start(f32[1,512]{1,0:T(1,128)} %stack_reshape.3) | copy-start | bytes 6148
  479.6 36.1 %copy-start.25 = (pred[32]{0:T(512)(128)(4,1)S(1)}, pred[32]{0:T(512)(128)(4,1)}, u32[]{:S(2)}) copy-start(pred[32]{0:T(512)(128)(4,1)} %get-tuple-element.10) | copy-start | bytes 100
  515.5 6.3 %copy-start.6 = (f32[256,496]{0,1:T(8,128)S(1)}, f32[256,496]{0,1:T(8,128)}, u32[]{:S(2)}) copy-start(f32[256,496]{0,1:T(8,128)} %get-tuple-element.27) | copy-start | bytes 1523716
  515.5 7.3 %copy-start.3 = (f32[256,511]{0,1:T(8,128)S(1)}, f32[256,511]{0,1:T(8,128)}, u32[]{:S(2)}) copy-start(f32[256,511]{0,1:T(8,128)} %get-tuple-element.24) | copy-start | bytes 1569796
  515.7 8.2 %copy-start.2 = (f32[256,511]{0,1:T(8,128)S(1)}, f32[256,511]{0,1:T(8,128)}, u32[]{:S(2)}) copy-start(f32[256,511]{0,1:T(8,128)} %get-tuple-element.25) | copy-start | bytes 1569796
  515.7 9.2 %collective-permute-start.1 = (f32[8,32,32]{2,1,0:T(8,128)S(1)}, f32[8,32,32]{2,1,0:T(8,128)S(1)}, u32[]{:S(2)}, u32[]{:S(2)}) collective-permute-start(f32[8,32,32]{2,1,0:T(8,128)S(1)} %bitcast_select_fusion), channel_id=1, source_target_pairs={{0,1},{1,0},{2,3},{3,2},{4,5},{5,4},{6,7},{7,6},{8,9},{9,8},{10,11... | collective-permute-start | bytes 98312 | tf_op jit(solution)/shard_map/ppermute | solution.py:22
  525.0 0.8 copy-start.9
  525.0 0.8 copy-start.11
  525.1 0.8 copy-start.14
  525.1 0.8 copy-start.15
where the time goes:
time: 535 us; the launch traced here: 529 us
  matrix products  244 us (46%)
  blocking collectives  116 us (22%)
  local copies, waits for them, and re-layouts  86.8 us (16%)
  other arithmetic  53.3 us (10%)
  starting transfers between devices  15.7 us (3%)
  waiting for transfers between devices  11.5 us (2%)
    dot_general x68, matrix products, apply(): return jnp.einsum(form, table, values, precision=HIGHEST)  212 us
    psum x2, blocking collectives, local(): flux = lax.psum(jnp.dot(weights, center, precision=HIGHEST), ('vel', 'sub'))  60.4 us
    unnamed x83, local copies, waits for them, and re-layouts  20 us
    add x2, other arithmetic, collide(): return cube + rate * (gain - cube * inverse(tables[2]))  17.1 us
    all_to_all x1, blocking collectives, local(): lax.all_to_all(post.reshape(count, count * count, 1, cells), 'vel', split...  17 us
    all_to_all x1, blocking collectives, local(): lax.all_to_all(state, 'vel', split_axis=2, concat_axis=1, tiled=True)  16.8 us
    dot_general x6, matrix products, inverse(): jnp.einsum(FORMS[2], cosine, second_real, precision=HIGHEST)  15.5 us
    dot_general x6, matrix products, inverse(): jnp.einsum(FORMS[2], sine_table, second_imag, precision=HIGHEST)  15 us
  transfers between devices with their start and end apart: 4, of which 2 were waited for; matrix products, arithmetic and copies ran while one was open for 7% of the time, Pallas kernels for 0%

commit v1 on v0

--- a/solution.py
+++ b/solution.py
@@ -3,6 +3,7 @@
 import jax.numpy as jnp
 from jax import lax
 from jax.sharding import PartitionSpec as P
+from jax.lax import all_gather
 
 VN = 16
 SY = 16
@@ -231,7 +232,8 @@
             tiled=True,
         )
         center = back.reshape(local_y * local_xz, total_cells)
-        flux = lax.psum(jnp.dot(weights, center, precision=HIGHEST), ("vel", "sub"))
+        x_local = jnp.dot(weights, center, precision=HIGHEST)
+        flux = all_gather(x_local, ("vel", "sub")).sum(axis=0)
         shaped = center.reshape(local_y, local_xz, total_cells)
         bottom_rows = jnp.take(shaped, bottom_index, axis=2)
         top_rows = shaped[:, :, height_count - 1 :: height_count]

time: 535 us -> 511 us (0.955)
  blocking collectives: 116 us -> 97.3 us
    psum x2 -> x0, blocking collectives: 60.4 us -> none  [local(): flux = lax.psum(jnp.dot(weights, center, precision=HIGHEST), ('vel', 'sub'))]
    all_gather x0 -> x2, blocking collectives: none -> 41.8 us  [local(): flux = all_gather(x_local, ('vel', 'sub')).sum(axis=0)]
where the time goes in v1:
time: 511 us; the launch traced here: 506 us
  matrix products  244 us (48%)
  blocking collectives  97.3 us (19%)
  local copies, waits for them, and re-layouts  86.8 us (17%)
  other arithmetic  54.1 us (11%)
  waiting for transfers between devices  11.5 us (2%)
  starting transfers between devices  10.6 us (2%)
    dot_general x68, matrix products, apply(): return jnp.einsum(form, table, values, precision=HIGHEST)  212 us
    all_gather x2, blocking collectives, local(): flux = all_gather(x_local, ('vel', 'sub')).sum(axis=0)  41.8 us
    unnamed x83, local copies, waits for them, and re-layouts  20 us
    add x2, other arithmetic, collide(): return cube + rate * (gain - cube * inverse(tables[2]))  17.1 us
    all_to_all x1, blocking collectives, local(): lax.all_to_all(post.reshape(count, count * count, 1, cells), 'vel', split...  17 us
    all_to_all x1, blocking collectives, local(): lax.all_to_all(state, 'vel', split_axis=2, concat_axis=1, tiled=True)  16.5 us
    dot_general x6, matrix products, inverse(): jnp.einsum(FORMS[2], cosine, second_real, precision=HIGHEST)  15.5 us
    dot_general x6, matrix products, inverse(): jnp.einsum(FORMS[2], sine_table, second_imag, precision=HIGHEST)  15 us
  transfers between devices with their start and end apart: 4, of which 2 were waited for; matrix products, arithmetic and copies ran while one was open for 7% of the time, Pallas kernels for 0%

profile of v1, /device:TPU:1, one launch (start us, length us, event | category | flops | bytes accessed | tf_op | source)
XLA Modules:
  0.0 505.7 jit_solution(16626522347718903397)
XLA Ops:
  3.6 6.4 %all-to-all-start = ((f32[8,1,16384]{2,1,0:T(1,128)}), f32[8,1,16384]{2,1,0:T(1,128)S(1)}, u32[]{:S(2)}, u32[]{:S(2)}) async-start(f32[8,1,16384]{2,1,0:T(1,128)} %reshape.621), calls=%async_computation | async-start | bytes 1048576 | tf_op jit(solution)/shard_map/all_to_all | solution.py:211
  19.5 3.9 all-to-all-done
  27.4 5.8 %all_to_all.132 = f32[8,256,64]{1,0,2:T(8,128)S(1)} all-to-all(f32[8,256,64]{1,0,2:T(8,128)S(1)} %copy.780), channel_id=1, replica_groups=mesh['groups'=2,'vel'=8,'sub'=2] {'sub'}, dimensions={2} | all-to-all | bytes 1048576 | tf_op jit(solution)/shard_map/all_to_all | solution.py:210
  38.6 3.3 fusion.158
  41.9 3.3 fusion.160
  45.2 3.5 subtract_bitcast_fusion.7
  53.7 3.4 add_bitcast_fusion.7
  60.0 3.4 multiply_bitcast_fusion.10
  72.4 3.4 fusion.134
  75.8 3.3 fusion.136
  88.1 3.4 fusion.102
  91.4 3.7 fusion.104
  103.9 3.5 fusion.118
  107.4 3.3 fusion.120
  113.7 3.3 subtract_bitcast_fusion.6
  117.1 3.5 add_bitcast_fusion.6
  128.6 3.8 subtract_bitcast_fusion.4
  132.4 3.4 add_bitcast_fusion.4
  144.0 3.4 subtract_bitcast_fusion.5
  147.4 3.3 add_bitcast_fusion.5
  155.9 8.6 %fusion.5 = f32[16,16,16,32]{3,0,2,1:T(8,128)} fusion(f32[16,16,16,32]{3,0,2,1:T(8,128)S(1)} %bitcast.352, f32[16,16,32,16]{2,3,1,0:T(8,128)S(1)} %fusion.23, f32[16,16,32,16]{2,3,1,0:T(8,128)S(1)} %fusion.25, f32[16,16,32,16]{2,3,1,0:T(8,128)S(1)} %fusion.29, f32[16,16,32,16]{2,3,1,0:T(8,128)S(1)} %fusion.31, f32[16,16,32,16]{2,3,1,0:T(8,128)S(1)} %fusion.34, ...), kind=kLoop, calls=%fused_computation.9 | loop fusion | flops 1441792 | bytes 4194304 | tf_op jit(solution)/shard_map/add | solution.py:179
  167.7 3.9 all-to-all-start.2
  177.5 7.6 %all-to-all-done.2 = f32[8,1,16384]{2,1,0:T(1,128)S(1)} async-done(((f32[8,1,16384]{2,1,0:T(1,128)}), f32[8,1,16384]{2,1,0:T(1,128)S(1)}, u32[]{:S(2)}, u32[]{:S(2)}) %all-to-all-start.2) | async-done | bytes 524320 | tf_op jit(solution)/shard_map/all_to_all | solution.py:222
  192.3 5.5 %all_to_all.133 = f32[2,1,65536]{2,1,0:T(1,128)S(1)} all-to-all(f32[2,1,65536]{2,1,0:T(1,128)S(1)} %reshape.625), channel_id=1, replica_groups=mesh['groups'=2,'vel'=8,'sub'=2] {'sub'}, dimensions={0} | all-to-all | bytes 1048576 | tf_op jit(solution)/shard_map/all_to_all | solution.py:221
  217.3 21.6 %all-gather.2 = f32[16,4,512]{2,1,0:T(4,128)} all-gather(f32[1,4,512]{2,1,0:T(4,128)S(1)} %convolution_bitcast_fusion.1), channel_id=2, replica_groups=mesh['groups'=2,'vel'=8,'sub'=2] {'vel','sub'}, dimensions={0}, use_global_device_ids=true | all-gather | bytes 139264 | tf_op jit(solution)/shard_map/all_gather | solution.py:236
  243.3 3.9 slice_divide_fusion.5
  257.9 3.3 fusion.253
  263.9 16.5 %all_to_all.134 = f32[8,1,16384]{2,1,0:T(1,128)S(1)} all-to-all(f32[8,1,16384]{2,1,0:T(1,128)S(1)} %reshape.627), channel_id=1, replica_groups=mesh['groups'=2,'vel'=8,'sub'=2] {'vel'}, dimensions={0} | all-to-all | bytes 1048576 | tf_op jit(solution)/shard_map/all_to_all | solution.py:211
  284.0 5.1 %all_to_all.135 = f32[8,256,64]{1,0,2:T(8,128)S(1)} all-to-all(f32[8,256,64]{1,0,2:T(8,128)S(1)} %copy.847), channel_id=1, replica_groups=mesh['groups'=2,'vel'=8,'sub'=2] {'sub'}, dimensions={2} | all-to-all | bytes 1048576 | tf_op jit(solution)/shard_map/all_to_all | solution.py:210
  294.5 3.4 fusion.94
  301.1 3.7 subtract_bitcast_fusion.3
  309.8 3.4 add_bitcast_fusion.3
  315.9 3.4 multiply_bitcast_fusion.4
  328.3 3.3 fusion.70
  337.9 3.3 fusion.48
  344.1 3.3 fusion.38
  347.5 3.5 fusion.40
  359.7 3.6 fusion.54
  369.6 3.3 subtract_bitcast_fusion.2
  373.0 3.7 add_bitcast_fusion.2
  384.7 3.6 subtract_bitcast_fusion
  388.3 3.4 add_bitcast_fusion
  399.9 3.4 subtract_bitcast_fusion.1
  403.3 3.3 add_bitcast_fusion.1
  412.0 8.6 %fusion.2 = f32[16,16,16,32]{3,0,2,1:T(8,128)} fusion(f32[16,16,16,32]{3,0,2,1:T(8,128)S(1)} %bitcast.349, f32[16,16,32,16]{2,3,1,0:T(8,128)S(1)} %fusion.7, f32[16,16,32,16]{2,3,1,0:T(8,128)S(1)} %fusion.9, f32[16,16,32,16]{2,3,1,0:T(8,128)S(1)} %fusion.13, f32[16,16,32,16]{2,3,1,0:T(8,128)S(1)} %fusion.15, f32[16,16,32,16]{2,3,1,0:T(8,128)S(1)} %fusion.18, ...), kind=kLoop, calls=%fused_computation.5 | loop fusion | flops 1441792 | bytes 4194304 | tf_op jit(solution)/shard_map/add | solution.py:179
  423.0 17.0 %all_to_all.136 = f32[8,1,16384]{2,1,0:T(1,128)S(1)} all-to-all(f32[8,1,16384]{2,1,0:T(1,128)S(1)} %reshape.629), channel_id=1, replica_groups=mesh['groups'=2,'vel'=8,'sub'=2] {'vel'}, dimensions={0} | all-to-all | bytes 1048576 | tf_op jit(solution)/shard_map/all_to_all | solution.py:222
  447.1 5.5 %all_to_all.137 = f32[2,1,65536]{2,1,0:T(1,128)S(1)} all-to-all(f32[2,1,65536]{2,1,0:T(1,128)S(1)} %reshape.631), channel_id=1, replica_groups=mesh['groups'=2,'vel'=8,'sub'=2] {'sub'}, dimensions={0} | all-to-all | bytes 1048576 | tf_op jit(solution)/shard_map/all_to_all | solution.py:221
  470.3 20.2 %all-gather.3 = f32[16,4,512]{2,1,0:T(4,128)S(1)} all-gather(f32[1,4,512]{2,1,0:T(4,128)S(1)} %convolution_bitcast_fusion), channel_id=3, replica_groups=mesh['groups'=2,'vel'=8,'sub'=2] {'vel','sub'}, dimensions={0}, use_global_device_ids=true | all-gather | bytes 139264 | tf_op jit(solution)/shard_map/all_gather | solution.py:236
  (245 shorter events, 250.9 us)
Async XLA Ops:
  1.8 11.1 %copy-start.33 = (s32[32]{0:T(128)S(1)}, s32[32]{0:T(128)}, u32[]{:S(2)}) copy-start(s32[32]{0:T(128)} %param.7) | copy-start | bytes 388
  1.8 11.1 %copy-start.12 = (s32[512]{0:T(512)S(1)}, s32[512]{0:T(512)}, u32[]{:S(2)}) copy-start(s32[512]{0:T(512)} %param.6) | copy-start | bytes 6148
  3.6 19.8 %all-to-all-start = ((f32[8,1,16384]{2,1,0:T(1,128)}), f32[8,1,16384]{2,1,0:T(1,128)S(1)}, u32[]{:S(2)}, u32[]{:S(2)}) async-start(f32[8,1,16384]{2,1,0:T(1,128)} %reshape.621), calls=%async_computation | async-start | bytes 1048576 | tf_op jit(solution)/shard_map/all_to_all | solution.py:211
  10.5 8.9 %copy-start.23 = (f32[8]{0:T(128)}, f32[8]{0:T(128)S(1)}, u32[]{:S(2)}) copy-start(f32[8]{0:T(128)S(1)} %get-tuple-element.71) | copy-start | bytes 100
  12.9 6.5 %copy-start.24 = (f32[32]{0:T(128)}, f32[32]{0:T(128)S(1)}, u32[]{:S(2)}) copy-start(f32[32]{0:T(128)S(1)} %get-tuple-element.67) | copy-start | bytes 388
  17.3 240.5 %copy-start.13 = (f32[512]{0:T(512)}, f32[512]{0:T(512)S(1)}, u32[]{:S(2)}) copy-start(f32[512]{0:T(512)S(1)} %sub.287) | copy-start | bytes 6148
  164.5 9.8 %copy-start.21 = (f32[496]{0:T(512)S(1)}, f32[496]{0:T(512)}, u32[]{:S(2)}) copy-start(f32[496]{0:T(512)} %get-tuple-element.55) | copy-start | bytes 5956
  164.5 9.8 %copy-start.22 = (f32[496]{0:T(512)S(1)}, f32[496]{0:T(512)}, u32[]{:S(2)}) copy-start(f32[496]{0:T(512)} %get-tuple-element.56) | copy-start | bytes 5956
  164.5 9.8 %copy-start.26 = (f32[16]{0:T(128)S(1)}, f32[16]{0:T(128)}, u32[]{:S(2)}) copy-start(f32[16]{0:T(128)} %get-tuple-element.53) | copy-start | bytes 196
  164.5 9.8 %copy-start.27 = (f32[16]{0:T(128)S(1)}, f32[16]{0:T(128)}, u32[]{:S(2)}) copy-start(f32[16]{0:T(128)} %get-tuple-element.54) | copy-start | bytes 196
  164.5 10.5 %copy-start.32 = (s32[32]{0:T(128)S(1)}, s32[32]{0:T(128)}, u32[]{:S(2)}) copy-start(s32[32]{0:T(128)} %get-tuple-element.11) | copy-start | bytes 388
  164.5 12.9 %copy-start.28 = (f32[8]{0:T(128)S(1)}, f32[8]{0:T(128)}, u32[]{:S(2)}) copy-start(f32[8]{0:T(128)} %get-tuple-element.72) | copy-start | bytes 100
  164.5 12.9 %copy-start.29 = (f32[32]{0:T(128)S(1)}, f32[32]{0:T(128)}, u32[]{:S(2)}) copy-start(f32[32]{0:T(128)} %get-tuple-element.63) | copy-start | bytes 388
  164.5 12.9 %copy-start.30 = (f32[32]{0:T(128)S(1)}, f32[32]{0:T(128)}, u32[]{:S(2)}) copy-start(f32[32]{0:T(128)} %get-tuple-element.64) | copy-start | bytes 388
  164.6 12.9 %copy-start.31 = (f32[32]{0:T(128)S(1)}, f32[32]{0:T(128)}, u32[]{:S(2)}) copy-start(f32[32]{0:T(128)} %get-tuple-element.68) | copy-start | bytes 388
  167.7 17.5 %all-to-all-start.2 = ((f32[8,1,16384]{2,1,0:T(1,128)}), f32[8,1,16384]{2,1,0:T(1,128)S(1)}, u32[]{:S(2)}, u32[]{:S(2)}) async-start(f32[8,1,16384]{2,1,0:T(1,128)} %reshape.623), calls=%async_computation.2 | async-start | bytes 1048576 | tf_op jit(solution)/shard_map/all_to_all | solution.py:222
  177.5 80.3 %copy-start.8 = (f32[8,32]{1,0:T(8,128)}, f32[8,32]{1,0:T(8,128)S(1)}, u32[]{:S(2)}) copy-start(f32[8,32]{1,0:T(8,128)S(1)} %get-tuple-element.57) | copy-start | bytes 3076
  177.5 80.3 %copy-start.10 = (f32[8,32]{1,0:T(8,128)}, f32[8,32]{1,0:T(8,128)S(1)}, u32[]{:S(2)}) copy-start(f32[8,32]{1,0:T(8,128)S(1)} %get-tuple-element.58) | copy-start | bytes 3076
  208.0 2.7 copy-start.1
  240.2 13.7 %copy-start.7 = (f32[256,496]{0,1:T(8,128)S(1)}, f32[256,496]{0,1:T(8,128)}, u32[]{:S(2)}) copy-start(f32[256,496]{0,1:T(8,128)} %get-tuple-element.33) | copy-start | bytes 1523716
  240.2 14.7 %copy-start.5 = (f32[256,511]{0,1:T(8,128)S(1)}, f32[256,511]{0,1:T(8,128)}, u32[]{:S(2)}) copy-start(f32[256,511]{0,1:T(8,128)} %get-tuple-element.30) | copy-start | bytes 1569796
  241.3 14.6 %copy-start.4 = (f32[256,511]{0,1:T(8,128)S(1)}, f32[256,511]{0,1:T(8,128)}, u32[]{:S(2)}) copy-start(f32[256,511]{0,1:T(8,128)} %get-tuple-element.31) | copy-start | bytes 1569796
  242.3 14.7 %collective-permute-start = (f32[8,32,32]{2,1,0:T(8,128)S(1)}, f32[8,32,32]{2,1,0:T(8,128)S(1)}, u32[]{:S(2)}, u32[]{:S(2)}) collective-permute-start(f32[8,32,32]{2,1,0:T(8,128)S(1)} %bitcast_select_fusion.1), channel_id=1, source_target_pairs={{0,1},{1,0},{2,3},{3,2},{4,5},{5,4},{6,7},{7,6},{8,9},{9,8},{10,11... | collective-permute-start | bytes 98312 | tf_op jit(solution)/shard_map/ppermute | solution.py:23
  460.8 2.2 copy-start.17
  460.8 2.2 copy-start.18
  460.8 2.2 copy-start.19
  460.8 2.2 copy-start.20
  463.5 2.1 copy-start
  468.3 22.4 %copy-start.16 = (f32[1,512]{1,0:T(1,128)S(1)}, f32[1,512]{1,0:T(1,128)}, u32[]{:S(2)}) copy-start(f32[1,512]{1,0:T(1,128)} %stack_reshape.3) | copy-start | bytes 6148
  468.3 26.4 %copy-start.25 = (pred[32]{0:T(512)(128)(4,1)S(1)}, pred[32]{0:T(512)(128)(4,1)}, u32[]{:S(2)}) copy-start(pred[32]{0:T(512)(128)(4,1)} %get-tuple-element.10) | copy-start | bytes 100
  494.6 3.7 copy-start.6
  494.6 4.7 copy-start.3
  494.7 5.6 %copy-start.2 = (f32[256,511]{0,1:T(8,128)S(1)}, f32[256,511]{0,1:T(8,128)}, u32[]{:S(2)}) copy-start(f32[256,511]{0,1:T(8,128)} %get-tuple-element.25) | copy-start | bytes 1569796
  494.8 6.6 %collective-permute-start.1 = (f32[8,32,32]{2,1,0:T(8,128)S(1)}, f32[8,32,32]{2,1,0:T(8,128)S(1)}, u32[]{:S(2)}, u32[]{:S(2)}) collective-permute-start(f32[8,32,32]{2,1,0:T(8,128)S(1)} %bitcast_select_fusion), channel_id=1, source_target_pairs={{0,1},{1,0},{2,3},{3,2},{4,5},{5,4},{6,7},{7,6},{8,9},{9,8},{10,11... | collective-permute-start | bytes 98312 | tf_op jit(solution)/shard_map/ppermute | solution.py:23
  501.5 0.8 copy-start.9
  501.5 0.8 copy-start.11
  501.5 0.8 copy-start.14
  501.5 0.8 copy-start.15
